TPU v7x, 128 devices: a whole 4x4x4 slice. The times are simulated.
128 devices in a mesh: ep: 32 (over y, z, core), tp: 4 (over x).
Axes of the slice: x: 4, y: 4, z: 4, core: 2. Of those that a mesh axis runs over, the one named last changes fastest.
Arguments:
- queries: bfloat16 [256, 64, 128], P('ep', 'tp'), may hold values from -115 to 115
- key_cache: bfloat16 [256, 4, 1024, 128], P('ep', 'tp'), may hold values from -6 to 6
- stored_value_cache: bfloat16 [256, 4, 1024, 128], P('ep', 'tp'), may hold values from -6 to 6
- new_key: bfloat16 [256, 4, 128], P('ep', 'tp'), may hold values from -4.5 to 4.5
- incoming_value: bfloat16 [256, 4, 128], P('ep', 'tp'), may hold values from -6 to 6
- lengths: int32 [256], P('ep'), may hold values from 1 to 1024, as said below
- policy: int32 [256, 4], P('ep', 'tp'), may hold values from 0 to 2
- retained_blocks: int32 [256, 4, 4], P('ep', 'tp'), may hold values from 0 to 15
- out_weight: bfloat16 [8192, 4096], P(None, 'ep'), may hold values from -0.5 to 0.5
- residual: bfloat16 [256, 4096], P(None, 'ep'), may hold values from -6 to 6
- norm_gain: float32 [4096], replicated, may hold values from 0.1 to 1.9
- routes: int32 [256, 8], replicated, may hold values from 0 to 63, all different within a row; in each aligned block of 256 rows (0 to 255, 256 to 511, ...) at most 64 rows name the same one
- router_logits: float32 [256, 8], replicated, may hold values from -6 to 6
- gate_weight: bfloat16 [64, 4096, 1536], P('ep', None, 'tp'), may hold values from -0.09375 to 0.09375
- up_weight: bfloat16 [64, 4096, 1536], P('ep', None, 'tp'), may hold values from -0.09375 to 0.09375
- down_weight: bfloat16 [64, 1536, 4096], P('ep', 'tp'), may hold values from -0.15625 to 0.15625
Outputs:
- mixed_out: bfloat16 [256, 4096], P(None, ('ep', 'tp'))
Inputs may be any that keep to these rules, and one draw needn't show every extreme that they name: `lengths`: each aligned group of 8 requests holds one of length 1024. At most 64 of all routes name one expert, a bound that some block reaches; a token names 8 different experts.
All inputs are finite; a program needn't handle non-finite values.
Results may differ from a plain program's by a relative error of at most 0.015.
Values may be sent and summed in bfloat16 or wider, within the bound.
A program may use at most 128 MiB of HBM per device.

v0:
```python
import jax
import jax.numpy as jnp
from jax import lax
from jax.sharding import PartitionSpec as P

TOPK = 8
EXP_DEV = 2
BLK = 64
BLOCK_COUNT = 16
WIN = 2
CONTEXT_SLOTS = 1024
CAP = 64
EPSILON = 1e-06


def token_keep(policy, retained_blocks, lengths):
    block_ids = jnp.arange(BLOCK_COUNT, dtype=jnp.int32)
    used_count = (lengths + BLK - 1) // BLK
    used_mask = block_ids < used_count[..., None]
    recent = block_ids >= (used_count - WIN)[..., None]
    last_block = block_ids == (used_count - 1)[..., None]
    listed = jnp.any(retained_blocks[..., :, None] == block_ids, axis=-2)
    policy_col = policy[..., None]
    block_keep = used_mask & (
        (policy_col == 0) & recent | (policy_col == 1) & (listed | last_block) | (policy_col == 2)
    )
    positions = jnp.arange(CONTEXT_SLOTS, dtype=jnp.int32)
    return jnp.repeat(block_keep, BLK, axis=-1) & (positions < lengths[..., None])


def per_device(
    queries,
    key_cache,
    stored_value_cache,
    new_key,
    incoming_value,
    lengths,
    policy,
    retained_blocks,
    out_weight,
    residual,
    norm_gain,
    routes,
    router_logits,
    gate_weight,
    up_weight,
    down_weight,
):
    ep_count = lax.axis_size("ep")
    tp_count = lax.axis_size("tp")
    request_count = queries.shape[0]
    group_heads = queries.shape[1]
    head_size = queries.shape[2]
    head_width = group_heads * head_size
    score_scale = head_size ** (-0.5)
    key_rows = key_cache[:, 0]
    value_rows = stored_value_cache[:, 0]
    own_key = new_key[:, 0]
    own_value = incoming_value[:, 0]
    kept_mask = token_keep(policy[:, 0], retained_blocks[:, 0], lengths)
    own_score = (
        jnp.einsum("rqd,rd->rq", queries, own_key, preferred_element_type=jnp.float32) * score_scale
    )
    scores = (
        jnp.einsum("rqd,rkd->rqk", queries, key_rows, preferred_element_type=jnp.float32)
        * score_scale
    )
    scores = jnp.where(kept_mask[:, None, :], scores, -jnp.inf)
    highest = jnp.maximum(jnp.max(scores, axis=-1), own_score)
    weights = jnp.exp(scores - highest[..., None])
    own_weight = jnp.exp(own_score - highest)
    totals = jnp.sum(weights, axis=-1) + own_weight
    own_low = lax.optimization_barrier(own_weight.astype(jnp.bfloat16)).astype(jnp.float32)
    weighted = jnp.einsum(
        "rqk,rkd->rqd", weights.astype(jnp.bfloat16), value_rows, preferred_element_type=jnp.float32
    )
    weighted = weighted + own_low[..., None] * own_value.astype(jnp.float32)[:, None, :]
    attended = (
        (weighted / totals[..., None]).astype(jnp.bfloat16).reshape(1, request_count, head_width)
    )
    column_count = out_weight.shape[1]
    all_requests = request_count * ep_count
    weight_parts = out_weight.reshape(tp_count, head_width, column_count)
    group_ids = jnp.arange(ep_count, dtype=jnp.int32)
    head_ids = jnp.arange(tp_count, dtype=jnp.int32)
    shard_rows = lax.all_gather(attended, ("ep", "tp"), axis=0, tiled=True)
    device_ids = jnp.arange(shard_rows.shape[0], dtype=jnp.int32)
    terms = jnp.einsum(
        "srk,tkc->strc", shard_rows, weight_parts, preferred_element_type=jnp.float32
    )
    head_match = (device_ids % tp_count)[:, None] == head_ids[None, :]
    chosen = jnp.sum(jnp.where(head_match[:, :, None, None], terms, 0.0), axis=1)
    group_match = (device_ids // tp_count)[:, None] == group_ids[None, :]
    added = jnp.sum(jnp.where(group_match[:, :, None, None], chosen[:, None], 0.0), axis=0)
    projected = added.reshape(all_requests, column_count)
    hidden = (residual.astype(jnp.float32) + projected).astype(jnp.bfloat16)
    experts_all = EXP_DEV * ep_count
    route_flat = routes.reshape(-1)
    onehot = (route_flat[:, None] == jnp.arange(experts_all, dtype=jnp.int32)[None, :]).astype(
        jnp.int32
    )
    route_rank = jnp.sum(jnp.cumsum(onehot, axis=0) * onehot, axis=1) - 1
    slot_index = route_flat * CAP + route_rank
    token_index = jnp.arange(route_flat.shape[0], dtype=jnp.int32) // TOPK
    outgoing_rows = (
        jnp.zeros((experts_all * CAP, column_count), jnp.bfloat16)
        .at[slot_index]
        .set(hidden[token_index])
    )
    arrived = lax.all_to_all(outgoing_rows, "ep", split_axis=0, concat_axis=1, tiled=True)
    rows_float = arrived.astype(jnp.float32)
    normed = (
        rows_float
        * lax.rsqrt(jnp.mean(rows_float * rows_float, axis=-1, keepdims=True) + EPSILON)
        * norm_gain
    ).astype(jnp.bfloat16)
    normed = normed.reshape(EXP_DEV, CAP, normed.shape[1])
    gate = jnp.einsum("ecd,edf->ecf", normed, gate_weight, preferred_element_type=jnp.float32)
    up_proj = jnp.einsum("ecd,edf->ecf", normed, up_weight, preferred_element_type=jnp.float32)
    act = (jax.nn.silu(gate) * up_proj).astype(jnp.bfloat16)
    partial_value = jnp.einsum("ecf,efd->ecd", act, down_weight, preferred_element_type=jnp.float32)
    partial_value = partial_value.reshape(1, EXP_DEV * CAP, partial_value.shape[2])
    returned = lax.all_to_all(
        lax.all_to_all(
            partial_value.astype(jnp.bfloat16), "ep", split_axis=2, concat_axis=1, tiled=True
        ),
        "tp",
        split_axis=2,
        concat_axis=0,
        tiled=True,
    ).astype(partial_value.dtype)
    summed = jnp.sum(returned, axis=0)
    route_weight = jax.nn.softmax(router_logits, axis=-1)
    narrow = summed.shape[1]
    picked_rows = summed[slot_index].reshape(-1, TOPK, narrow)
    mixture = jnp.sum(picked_rows * route_weight[..., None], axis=1)
    tp_index_out = lax.axis_index("tp")
    base_rows = lax.dynamic_slice_in_dim(hidden, tp_index_out * narrow, narrow, 1)
    return (base_rows.astype(jnp.float32) + mixture).astype(jnp.bfloat16)


def solution(mesh):
    return jax.shard_map(
        per_device,
        mesh=mesh,
        in_specs=(
            P("ep", "tp", None),
            P("ep", "tp", None, None),
            P("ep", "tp", None, None),
            P("ep", "tp", None),
            P("ep", "tp", None),
            P("ep"),
            P("ep", "tp"),
            P("ep", "tp", None),
            P(None, "ep"),
            P(None, "ep"),
            P(),
            P(),
            P(),
            P("ep", None, "tp"),
            P("ep", None, "tp"),
            P("ep", "tp", None),
        ),
        out_specs=P(None, ("ep", "tp")),
        check_vma=False,
    )
```

profile of v0, /device:TPU:1, one launch (start us, length us, event | category | flops | bytes accessed | tf_op | source)
XLA Modules:
  0.0 263.7 jit_solution(4339838347839793135)
XLA Ops:
  6.5 0.8 broadcast_add_fusion.2
  7.4 0.7 compare_bitcast_fusion.2
  8.0 0.8 fusion.44
  8.8 0.1 fusion.49
  8.9 0.1 broadcast_in_dim.43
  9.0 0.1 reshape.254
  9.1 0.9 fusion.43
  10.0 0.9 fusion.47
  10.8 2.4 fusion.58
  13.2 0.2 fusion.32
  13.5 0.4 fusion.22
  13.9 0.6 reshape.255
  14.6 0.0 all-gather.2.cloned.1.call-update
  14.6 0.1 copy.114
  14.7 0.1 eq.115
  14.8 0.1 eq.111
  15.0 0.1 copy.109
  15.1 18.1 %reduce-window.6 = s32[64,16,128]{2,1,0:T(8,128)S(1)} reduce-window(s32[64,16,128]{2,1,0:T(8,128)S(1)} %fusion.31, s32[]{:T(128)} %constant.89.clone.1), window={size=1x1x128 pad=0_0x0_0x127_0}, to_apply=%region_5.6 | reduce-window | flops 16646144 | bytes 1048580 | tf_op jit(solution)/shard_map/reduce-window
  33.3 0.2 slice.12
  33.5 0.4 copy.132
  33.9 0.2 reduce-window.9
  34.1 0.1 copy.113
  34.2 0.1 mul.102
  34.4 0.2 broadcast_add_fusion
  34.6 0.2 fusion.27
  34.8 0.1 iota_compare_fusion.2
  35.0 50.4 %all-gather.2.cloned.1.call-done = bf16[128,8,2048]{2,1,0:T(8,128)(2,1)} async-done(((bf16[1,8,2048]{2,1,0:T(8,128)(2,1)}), bf16[128,8,2048]{2,1,0:T(8,128)(2,1)}) %all-gather.2.cloned.1.call-update) | async-done | bytes 4194320 | tf_op jit(solution)/shard_map/all_gather | solution.py:86
  85.4 7.0 %select_reduce_fusion.1 = f32[128,8,128]{2,0,1:T(8,128)S(1)} fusion(bf16[4,2048,128,1]{2,1,0,3:T(8,128)(2,1)S(1)} %bitcast.80, bf16[128,8,2048,1]{2,1,0,3:T(8,128)(2,1)} %bitcast.101, pred[128,4]{0,1:T(4,128)(4,1)S(1)} %iota_compare_fusion.8), kind=kOutput, calls=%fused_computation.16 | convolution fusion | flops 2148401152 | bytes 6816256 | tf_op jit(solution)/shard_map/srk,tkc->strc/dot_general | solution.py:88
  92.4 0.3 copy.111
  92.7 5.6 %select_reduce_fusion = f32[32,8,128]{2,1,0:T(8,128)S(1)} fusion(f32[128,8,128]{2,1,0:T(8,128)S(1)} %copy.111, pred[128,32]{1,0:T(8,128)(4,1)S(1)} %iota_compare_fusion.2), kind=kLoop, calls=%fused_computation.3 | loop fusion | flops 8355840 | bytes 659456 | tf_op jit(solution)/shard_map/reduce_sum | solution.py:94
  98.2 0.1 copy.112
  98.4 0.1 copy.118
  98.5 12.9 %scatter_custom_fusion = bf16[4096,128]{1,0:T(8,128)(2,1)} fusion(s32[2048]{0:T(1024)S(1)} %bitcast.94, bf16[256,128]{1,0:T(8,128)(2,1)S(1)} %copy.118, s32[2048]{0:T(1024)S(1)} %broadcast_clamp_fusion.1, bf16[]{:T(256)} %constant.103.clone.1), kind=kCustom, calls=%fused_computation.29 | custom fusion | bytes 1048578 | tf_op jit(solution)/shard_map/scatter | solution.py:108
  111.4 21.7 %all_to_all.40 = bf16[32,128,128]{2,1,0:T(8,128)(2,1)S(1)} all-to-all(bf16[32,128,128]{2,1,0:T(8,128)(2,1)} %bitcast.89), channel_id=1, replica_groups=mesh['ep'=32,'tp'=4] {'ep'}, dimensions={0} | all-to-all | bytes 2097152 | tf_op jit(solution)/shard_map/all_to_all | solution.py:110
  133.1 0.2 convert_bitcast_fusion
  133.3 2.6 copy.119
  135.9 2.7 %reshape.261 = f32[2,64,4096]{2,1,0:T(8,128)} reshape(f32[128,32,128]{2,1,0:T(8,128)} %copy.119) | data formatting | bytes 4194304 | tf_op jit(solution)/shard_map/convert_element_type | solution.py:111
  138.6 0.3 fusion.2
  138.9 0.1 rsqrt.12
  139.0 4.5 %fusion.34 = f32[2,64,384]{2,1,0:T(8,128)S(1)} fusion(bf16[2,4096,384]{2,1,0:T(8,128)(2,1)} %param.29, f32[2,64,4096]{2,1,0:T(8,128)} %reshape.261, f32[4096]{0:T(1024)S(1)} %copy-done.2, f32[2,64]{1,0:T(2,128)S(1)} %rsqrt.12), kind=kOutput, calls=%fused_computation.38 | convolution fusion | flops 404226048 | bytes 8602112 | tf_op jit(solution)/shard_map/ecd,edf->ecf/dot_general | solution.py:118
  143.6 7.2 %convolution_convert_fusion = bf16[2,64,4096]{2,1,0:T(8,128)(2,1)S(1)} fusion(bf16[2,384,4096]{2,1,0:T(8,128)(2,1)} %param.31, bf16[2,4096,384]{2,1,0:T(8,128)(2,1)} %param.30, f32[2,64,4096]{2,1,0:T(8,128)} %reshape.261, f32[4096]{0:T(1024)S(1)} %copy-done.2, f32[2,64]{1,0:T(2,128)S(1)} %rsqrt.12, f32[2,64,384]{2,1,0:T(8,128)S(1)} %fusion.34), kind=kOutput, calls=%fused_computation.4 | convolution fusion | flops 807698432 | bytes 15942144 | tf_op jit(solution)/shard_map/ecf,efd->ecd/dot_general | solution.py:121
  150.7 3.9 %copy.120 = bf16[1,128,4096]{1,0,2:T(2,128)(2,1)} copy(bf16[1,128,4096]{2,1,0:T(8,128)(2,1)S(1)} %bitcast.85) | data formatting | bytes 2097152 | tf_op jit(solution)/shard_map/convert_element_type | solution.py:125
  154.6 0.5 broadcast.308
  155.1 23.4 %reduce.6 = bf16[4096,128]{1,0:T(8,128)(2,1)S(1)} reduce(bf16[4096,1,128]{2,1,0:T(2,128)(2,1)} %bitcast.83, bf16[]{:T(256)} %broadcast.308), dimensions={1}, to_apply=%bitcast.67.reduce_sub_computation | reduce | bytes 2097154
  178.6 1.1 reshape.297
  179.7 20.9 %all_to_all.41 = bf16[32,2,8192]{2,1,0:T(2,128)(2,1)S(1)} all-to-all(bf16[32,2,8192]{2,1,0:T(2,128)(2,1)} %reshape.297), channel_id=1, replica_groups=mesh['ep'=32,'tp'=4] {'ep'}, dimensions={0} | all-to-all | bytes 2097152 | tf_op jit(solution)/shard_map/all_to_all | solution.py:124
  200.6 3.5 %reshape.298 = bf16[4096,1,128]{2,1,0:T(2,128)(2,1)} reshape(bf16[32,2,8192]{2,1,0:T(2,128)(2,1)S(1)} %all_to_all.41) | data formatting | bytes 2097152
  204.0 1.7 copy.133
  205.7 1.3 copy.121
  207.1 5.5 %copy.122 = bf16[1,4096,128]{1,0,2:T(2,128)(2,1)} copy(bf16[1,4096,128]{2,1,0:T(8,128)(2,1)} %bitcast.87) | data formatting | bytes 2097152 | tf_op jit(solution)/shard_map/all_to_all | solution.py:124
  212.6 8.4 %reduce.7 = bf16[128,4096]{1,0:T(8,128)(2,1)S(1)} reduce(bf16[128,1,4096]{2,1,0:T(2,128)(2,1)} %bitcast.84, bf16[]{:T(256)} %broadcast.308), dimensions={1}, to_apply=%bitcast.69.reduce_sub_computation | reduce | bytes 2097154
  220.9 0.0 copy-start.3
  221.0 2.0 reshape.299
  223.0 3.5 %all-to-all-start.2 = ((bf16[4,2,65536]{2,1,0:T(2,128)(2,1)}), bf16[4,2,65536]{2,1,0:T(2,128)(2,1)S(1)}, u32[]{:S(2)}, u32[]{:S(2)}) async-start(bf16[4,2,65536]{2,1,0:T(2,128)(2,1)} %reshape.299), calls=%async_computation.2 | async-start | bytes 2097152 | tf_op jit(solution)/shard_map/all_to_all | solution.py:123
  226.6 0.1 copy.125
  226.7 14.8 %all-to-all-done.2 = bf16[4,2,65536]{2,1,0:T(2,128)(2,1)S(1)} async-done(((bf16[4,2,65536]{2,1,0:T(2,128)(2,1)}), bf16[4,2,65536]{2,1,0:T(2,128)(2,1)S(1)}, u32[]{:S(2)}, u32[]{:S(2)}) %all-to-all-start.2) | async-done | bytes 1048608 | tf_op jit(solution)/shard_map/all_to_all | solution.py:123
  241.5 2.3 reshape.300
  243.9 2.7 %copy.123 = bf16[1,4096,128]{1,2,0:T(8,128)(2,1)S(1)} copy(bf16[1,4096,128]{1,0,2:T(2,128)(2,1)} %bitcast.82) | data formatting | bytes 2097152 | tf_op jit(solution)/shard_map/all_to_all | solution.py:123
  246.6 0.2 convert_reduce_fusion
  246.8 2.0 copy.124
  248.7 7.0 %gather_fusion = f32[2048,32]{1,0:T(8,128)S(1)} fusion(f32[4096,32]{1,0:T(8,128)} %copy.124, s32[2048]{0:T(1024)S(1)} %broadcast_clamp_fusion), kind=kCustom, calls=%fused_computation.1 | custom fusion | bytes 532480 | tf_op jit(solution)/shard_map/gather | solution.py:135
  255.8 0.4 fusion.25
  256.2 0.1 copy.126
  256.2 0.6 add_convert_fusion.1
  (34 shorter events, 0.2 us)
Async XLA Ops:
  6.5 78.8 %copy-start = (bf16[8192,128]{1,0:T(8,128)(2,1)S(1)}, bf16[8192,128]{1,0:T(8,128)(2,1)}, u32[]{:S(2)}) copy-start(bf16[8192,128]{1,0:T(8,128)(2,1)} %param.24) | copy-start | bytes 6291460
  6.5 6.9 %copy-start.6 = (bf16[8,1,128]{2,0,1:T(8,128)(2,1)S(1)}, bf16[8,1,128]{2,0,1:T(8,128)(2,1)}, u32[]{:S(2)}) copy-start(bf16[8,1,128]{2,0,1:T(8,128)(2,1)} %param.20) | copy-start | bytes 6148
  6.5 78.8 %all-gather.2.cloned.1.call-start = ((), (), s32[]{:S(2)}) async-start(), calls=%async_computation.3 | async-start | bytes 4227072 | tf_op jit(solution)/shard_map/all_gather | solution.py:86
  9.1 4.4 %copy-start.1 = (bf16[8,1,1024,128]{3,2,1,0:T(8,128)(2,1)S(1)}, bf16[8,1,1024,128]{3,2,1,0:T(8,128)(2,1)}, u32[]{:S(2)}) copy-start(bf16[8,1,1024,128]{3,2,1,0:T(8,128)(2,1)} %param.18) | copy-start | bytes 6291460
  13.2 1.4 copy-start.5
  13.2 1.8 copy-start.4
  135.9 3.1 %copy-start.2 = (f32[4096]{0:T(1024)S(1)}, f32[4096]{0:T(1024)}, u32[]{:S(2)}) copy-start(f32[4096]{0:T(1024)} %param.26) | copy-start | bytes 49156
  220.9 5.5 %copy-start.3 = (f32[256,8]{0,1:T(8,128)S(1)}, f32[256,8]{0,1:T(8,128)}, u32[]{:S(2)}) copy-start(f32[256,8]{0,1:T(8,128)} %param.28) | copy-start | bytes 24580
  223.0 18.6 %all-to-all-start.2 = ((bf16[4,2,65536]{2,1,0:T(2,128)(2,1)}), bf16[4,2,65536]{2,1,0:T(2,128)(2,1)S(1)}, u32[]{:S(2)}, u32[]{:S(2)}) async-start(bf16[4,2,65536]{2,1,0:T(2,128)(2,1)} %reshape.299), calls=%async_computation.2 | async-start | bytes 2097152 | tf_op jit(solution)/shard_map/all_to_all | solution.py:123
Sparse Core Ops, SparseCore 0:
  14.7 70.6 all-gather.1
where the time goes:
time: 265 us; the launch traced here: 264 us
  waiting for transfers between devices  65.3 us (25%)
  other arithmetic  61.5 us (23%)
  local copies, waits for them, and re-layouts  54.8 us (21%)
  blocking collectives  42.5 us (16%)
  matrix products  22.3 us (8%)
  between operations  13.8 us (5%)
  starting transfers between devices  3.52 us (1%)
    all_gather x1, waiting for transfers between devices, per_device(): shard_rows = lax.all_gather(attended, ('ep', 'tp'), axis=0, tiled=True)  50.4 us
    unnamed x2, other arithmetic  31.8 us
    all_to_all x1, blocking collectives, per_device(): lax.all_to_all(outgoing_rows, 'ep', split_axis=0, concat_axis=1, tiled=True)  21.7 us
    all_to_all x1, blocking collectives, per_device(): lax.all_to_all(partial_value.astype(jnp.bfloat16), 'ep', split_axis=2, co...  20.9 us
    another operation x3, other arithmetic  18.5 us
    all_to_all x1, waiting for transfers between devices, per_device(): lax.all_to_all(lax.all_to_all(partial_value.astype(jnp.bfloat16), 'ep', s...  14.8 us
    scatter x1, local copies, waits for them, and re-layouts, per_device(): outgoing_rows = jnp.zeros((experts_all * CAP, column_count), jnp.bfloat16...  12.9 us
    unnamed x22, local copies, waits for them, and re-layouts  11.4 us
  transfers between devices with their start and end apart: 2, of which 2 were waited for; matrix products, arithmetic and copies ran while one was open for 8% of the time, Pallas kernels for 0%

commit v1 on v0

--- a/solution.py
+++ b/solution.py
@@ -83,7 +83,10 @@
     weight_parts = out_weight.reshape(tp_count, head_width, column_count)
     group_ids = jnp.arange(ep_count, dtype=jnp.int32)
     head_ids = jnp.arange(tp_count, dtype=jnp.int32)
-    shard_rows = lax.all_gather(attended, ("ep", "tp"), axis=0, tiled=True)
+    shard_rows = jnp.concatenate(
+        lax.all_to_all(jnp.stack([attended] * lax.axis_size(("ep", "tp"))), ("ep", "tp"), 0, 0),
+        axis=0,
+    )
     device_ids = jnp.arange(shard_rows.shape[0], dtype=jnp.int32)
     terms = jnp.einsum(
         "srk,tkc->strc", shard_rows, weight_parts, preferred_element_type=jnp.float32

time: 265 us -> 231 us (0.87)
  waiting for transfers between devices: 65.3 us -> 47.6 us
  between operations: 13.8 us -> 0.44 us
  starting transfers between devices: 3.52 us -> 15.5 us
  local copies, waits for them, and re-layouts: 54.8 us -> 45.5 us
    all_gather x1 -> x0, waiting for transfers between devices: 50.4 us -> none  [per_device(): shard_rows = lax.all_gather(attended, ('ep', 'tp'), axis=0, tiled=True)]
    all_to_all x0 -> x1, waiting for transfers between devices: none -> 32.7 us  [per_device(): lax.all_to_all(jnp.stack([attended] * lax.axis_size(('ep', 'tp'))), ('ep'...]
    all_to_all x0 -> x1, starting transfers between devices: none -> 12 us  [per_device(): lax.all_to_all(jnp.stack([attended] * lax.axis_size(('ep', 'tp'))), ('ep'...]
    unnamed x22 -> x25, local copies, waits for them, and re-layouts: 11.4 us -> 5.19 us
  transfers between devices with their start and end apart: 2 -> 2, of which waited for: 2 -> 2; matrix products, arithmetic and copies ran while one was open for 8% -> 9% of each run, Pallas kernels for 0% -> 0%
where the time goes in v1:
time: 231 us; the launch traced here: 230 us
  other arithmetic  59.1 us (26%)
  waiting for transfers between devices  47.6 us (21%)
  local copies, waits for them, and re-layouts  45.5 us (20%)
  blocking collectives  40.6 us (18%)
  matrix products  21.1 us (9%)
  starting transfers between devices  15.5 us (7%)
    all_to_all x1, waiting for transfers between devices, per_device(): lax.all_to_all(jnp.stack([attended] * lax.axis_size(('ep', 'tp'))), ('ep'...  32.7 us
    unnamed x2, other arithmetic  29.4 us
    all_to_all x1, blocking collectives, per_device(): lax.all_to_all(partial_value.astype(jnp.bfloat16), 'ep', split_axis=2, co...  20.7 us
    all_to_all x1, blocking collectives, per_device(): lax.all_to_all(outgoing_rows, 'ep', split_axis=0, concat_axis=1, tiled=True)  20 us
    another operation x3, other arithmetic  18.5 us
    all_to_all x1, waiting for transfers between devices, per_device(): lax.all_to_all(lax.all_to_all(partial_value.astype(jnp.bfloat16), 'ep', s...  14.8 us
    scatter x1, local copies, waits for them, and re-layouts, per_device(): outgoing_rows = jnp.zeros((experts_all * CAP, column_count), jnp.bfloat16...  12.2 us
    all_to_all x1, starting transfers between devices, per_device(): lax.all_to_all(jnp.stack([attended] * lax.axis_size(('ep', 'tp'))), ('ep'...  12 us
  transfers between devices with their start and end apart: 2, of which 2 were waited for; matrix products, arithmetic and copies ran while one was open for 9% of the time, Pallas kernels for 0%

profile of v1, /device:TPU:1, one launch (start us, length us, event | category | flops | bytes accessed | tf_op | source)
XLA Modules:
  0.0 229.8 jit_solution(12641125462949882447)
XLA Ops:
  0.0 0.8 broadcast_add_fusion.2
  0.8 0.7 compare_bitcast_fusion.2
  1.5 0.8 fusion.48
  2.3 0.1 fusion.53
  2.3 0.1 broadcast_in_dim.43
  2.4 0.1 reshape.258
  2.5 0.0 copy-start.2
  2.5 0.9 fusion.47
  3.4 0.9 fusion.51
  4.3 2.4 %fusion.62 = (f32[8,16]{1,0:T(8,128)S(1)}, f32[8,16,1024]{2,1,0:T(8,128)S(1)}) fusion(bf16[8,16,128]{2,1,0:T(8,128)(2,1)} %param.16, bf16[8,1,1024,128]{3,2,1,0:T(8,128)(2,1)} %param.17, pred[8,1024]{1,0:T(8,128)(4,1)S(1)} %fusion.47), kind=kOutput, calls=%fused_computation.103 | convolution fusion | flops 33947520 | bytes 2662912 | tf_op jit(solution)/shard_map/rqd,rkd->rqk/dot_general | solution.py:65
  6.7 0.2 fusion.36
  7.0 0.4 fusion.26
  7.4 2.5 %stack.3 = bf16[128,1,8,2048]{3,2,1,0:T(8,128)(2,1)} broadcast(bf16[8,2048]{1,0:T(8,128)(2,1)S(1)} %bitcast.106), dimensions={2,3} | broadcast | bytes 4227072 | tf_op jit(solution)/shard_map/stack | solution.py:87
  9.9 12.0 %all-to-all-start = ((bf16[128,1,8,2048]{3,2,1,0:T(8,128)(2,1)}), bf16[128,1,8,2048]{3,2,1,0:T(8,128)(2,1)}, u32[]{:S(2)}, u32[]{:S(2)}) async-start(bf16[128,1,8,2048]{3,2,1,0:T(8,128)(2,1)} %stack.3), calls=%async_computation | async-start | bytes 8388608 | tf_op jit(solution)/shard_map/all_to_all | solution.py:87
  21.9 0.1 copy.111
  22.0 0.1 eq.115
  22.1 0.1 eq.111
  22.3 0.1 copy.106
  22.4 18.1 %reduce-window.6 = s32[64,16,128]{2,1,0:T(8,128)S(1)} reduce-window(s32[64,16,128]{2,1,0:T(8,128)S(1)} %fusion.35, s32[]{:T(128)} %constant.89.clone.1), window={size=1x1x128 pad=0_0x0_0x127_0}, to_apply=%region_5.6 | reduce-window | flops 16646144 | bytes 1048580 | tf_op jit(solution)/shard_map/reduce-window
  40.6 0.2 slice.12
  40.8 0.4 copy.127
  41.2 0.2 reduce-window.9
  41.4 0.1 copy.110
  41.5 0.1 mul.102
  41.7 0.2 broadcast_add_fusion
  41.9 0.2 fusion.31
  42.1 0.1 iota_compare_fusion.2
  42.3 32.7 %all-to-all-done = bf16[128,1,8,2048]{3,2,1,0:T(8,128)(2,1)} async-done(((bf16[128,1,8,2048]{3,2,1,0:T(8,128)(2,1)}), bf16[128,1,8,2048]{3,2,1,0:T(8,128)(2,1)}, u32[]{:S(2)}, u32[]{:S(2)}) %all-to-all-start) | async-done | bytes 4194336 | tf_op jit(solution)/shard_map/all_to_all | solution.py:87
  75.0 7.0 %select_reduce_fusion.1 = f32[128,8,128]{2,0,1:T(8,128)S(1)} fusion(bf16[4,2048,128,1]{2,1,0,3:T(8,128)(2,1)S(1)} %bitcast.94, bf16[128,1,8,2048]{3,2,1,0:T(8,128)(2,1)} %all-to-all-done, pred[128,4]{0,1:T(4,128)(4,1)S(1)} %iota_compare_fusion.8), kind=kOutput, calls=%fused_computation.17 | convolution fusion | flops 2148401152 | bytes 6816256 | tf_op jit(solution)/shard_map/srk,tkc->strc/dot_general | solution.py:91
  82.0 0.3 copy.108
  82.3 5.6 %select_reduce_fusion = f32[32,8,128]{2,1,0:T(8,128)S(1)} fusion(f32[128,8,128]{2,1,0:T(8,128)S(1)} %copy.108, pred[128,32]{1,0:T(8,128)(4,1)S(1)} %iota_compare_fusion.2), kind=kLoop, calls=%fused_computation.3 | loop fusion | flops 8355840 | bytes 659456 | tf_op jit(solution)/shard_map/reduce_sum | solution.py:97
  87.9 0.1 copy.109
  88.0 0.1 copy.115
  88.1 12.2 %scatter_custom_fusion = bf16[4096,128]{1,0:T(8,128)(2,1)S(1)} fusion(s32[2048]{0:T(1024)S(1)} %bitcast.109, bf16[256,128]{1,0:T(8,128)(2,1)S(1)} %copy.115, s32[2048]{0:T(1024)S(1)} %broadcast_clamp_fusion.1, bf16[]{:T(256)} %constant.103.clone.1), kind=kCustom, calls=%fused_computation.31 | custom fusion | bytes 1048578 | tf_op jit(solution)/shard_map/scatter | solution.py:111
  100.3 20.0 %all_to_all.45 = bf16[32,128,128]{2,1,0:T(8,128)(2,1)S(1)} all-to-all(bf16[32,128,128]{2,1,0:T(8,128)(2,1)S(1)} %bitcast.103), channel_id=1, replica_groups=mesh['ep'=32,'tp'=4] {'ep'}, dimensions={0} | all-to-all | bytes 2097152 | tf_op jit(solution)/shard_map/all_to_all | solution.py:113
  120.3 0.2 convert_bitcast_fusion
  120.5 2.6 %copy.116 = f32[128,32,128]{2,1,0:T(8,128)} copy(f32[128,32,128]{2,0,1:T(8,128)S(1)} %convert_bitcast_fusion) | data formatting | bytes 4194304 | tf_op jit(solution)/shard_map/convert_element_type | solution.py:114
  123.1 1.8 reshape.265
  124.8 0.3 fusion.3
  125.1 0.1 rsqrt.12
  125.2 3.9 %fusion.38 = f32[2,64,384]{2,1,0:T(8,128)S(1)} fusion(bf16[2,4096,384]{2,1,0:T(8,128)(2,1)} %param.29, f32[2,64,4096]{2,1,0:T(8,128)S(1)} %reshape.265, f32[4096]{0:T(1024)S(1)} %copy-done.3, f32[2,64]{1,0:T(2,128)S(1)} %rsqrt.12), kind=kOutput, calls=%fused_computation.40 | convolution fusion | flops 404226048 | bytes 8602112 | tf_op jit(solution)/shard_map/ecd,edf->ecf/dot_general | solution.py:121
  129.1 6.6 %convolution_convert_fusion = bf16[2,64,4096]{2,1,0:T(8,128)(2,1)S(1)} fusion(bf16[2,384,4096]{2,1,0:T(8,128)(2,1)} %param.31, bf16[2,4096,384]{2,1,0:T(8,128)(2,1)} %param.30, f32[2,64,4096]{2,1,0:T(8,128)S(1)} %reshape.265, f32[4096]{0:T(1024)S(1)} %copy-done.3, f32[2,64]{1,0:T(2,128)S(1)} %rsqrt.12, f32[2,64,384]{2,1,0:T(8,128)S(1)} %fusion.38), kind=kOutput, calls=%fused_computation.4 | convolution fusion | flops 807698432 | bytes 15942144 | tf_op jit(solution)/shard_map/ecf,efd->ecd/dot_general | solution.py:124
  135.7 2.8 %copy.117 = bf16[1,128,4096]{1,0,2:T(2,128)(2,1)S(1)} copy(bf16[1,128,4096]{2,1,0:T(8,128)(2,1)S(1)} %bitcast.99) | data formatting | bytes 2097152 | tf_op jit(solution)/shard_map/convert_element_type | solution.py:128
  138.5 0.5 broadcast.310
  139.1 22.4 %reduce.6 = bf16[4096,128]{1,0:T(8,128)(2,1)S(1)} reduce(bf16[4096,1,128]{2,1,0:T(2,128)(2,1)S(1)} %bitcast.97, bf16[]{:T(256)} %broadcast.310), dimensions={1}, to_apply=%bitcast.80.reduce_sub_computation | reduce | bytes 2097154
  161.4 0.3 reshape.301
  161.7 20.7 %all_to_all.46 = bf16[32,2,8192]{2,1,0:T(2,128)(2,1)S(1)} all-to-all(bf16[32,2,8192]{2,1,0:T(2,128)(2,1)S(1)} %reshape.301), channel_id=1, replica_groups=mesh['ep'=32,'tp'=4] {'ep'}, dimensions={0} | all-to-all | bytes 2097152 | tf_op jit(solution)/shard_map/all_to_all | solution.py:127
  182.4 1.0 reshape.302
  183.4 0.1 copy.128
  183.6 1.3 copy.118
  184.9 4.7 %copy.119 = bf16[1,4096,128]{1,0,2:T(2,128)(2,1)S(1)} copy(bf16[1,4096,128]{2,1,0:T(8,128)(2,1)} %bitcast.101) | data formatting | bytes 2097152 | tf_op jit(solution)/shard_map/all_to_all | solution.py:127
  189.7 7.0 %reduce.7 = bf16[128,4096]{1,0:T(8,128)(2,1)S(1)} reduce(bf16[128,1,4096]{2,1,0:T(2,128)(2,1)S(1)} %bitcast.98, bf16[]{:T(256)} %broadcast.310), dimensions={1}, to_apply=%bitcast.82.reduce_sub_computation | reduce | bytes 2097154
  196.7 2.0 reshape.303
  198.7 3.5 %all-to-all-start.3 = ((bf16[4,2,65536]{2,1,0:T(2,128)(2,1)}), bf16[4,2,65536]{2,1,0:T(2,128)(2,1)S(1)}, u32[]{:S(2)}, u32[]{:S(2)}) async-start(bf16[4,2,65536]{2,1,0:T(2,128)(2,1)} %reshape.303), calls=%async_computation.3 | async-start | bytes 2097152 | tf_op jit(solution)/shard_map/all_to_all | solution.py:126
  202.3 0.1 copy.122
  202.4 14.8 %all-to-all-done.3 = bf16[4,2,65536]{2,1,0:T(2,128)(2,1)S(1)} async-done(((bf16[4,2,65536]{2,1,0:T(2,128)(2,1)}), bf16[4,2,65536]{2,1,0:T(2,128)(2,1)S(1)}, u32[]{:S(2)}, u32[]{:S(2)}) %all-to-all-start.3) | async-done | bytes 1048608 | tf_op jit(solution)/shard_map/all_to_all | solution.py:126
  217.3 0.9 reshape.304
  218.2 1.1 copy.120
  219.4 0.2 convert_reduce_fusion
  219.6 2.0 copy.121
  221.5 7.2 %gather_fusion = f32[2048,32]{1,0:T(8,128)S(1)} fusion(f32[4096,32]{1,0:T(8,128)} %copy.121, s32[2048]{0:T(1024)S(1)} %broadcast_clamp_fusion), kind=kCustom, calls=%fused_computation.1 | custom fusion | bytes 532480 | tf_op jit(solution)/shard_map/gather | solution.py:138
  228.7 0.4 fusion.29
  229.1 0.1 copy.123
  229.2 0.6 add_convert_fusion.1
  (36 shorter events, 0.2 us)
Async XLA Ops:
  0.0 75.0 %copy-start = (bf16[8192,128]{1,0:T(8,128)(2,1)S(1)}, bf16[8192,128]{1,0:T(8,128)(2,1)}, u32[]{:S(2)}) copy-start(bf16[8192,128]{1,0:T(8,128)(2,1)} %param.24) | copy-start | bytes 6291460
  0.0 6.9 %copy-start.7 = (bf16[8,1,128]{2,0,1:T(8,128)(2,1)S(1)}, bf16[8,1,128]{2,0,1:T(8,128)(2,1)}, u32[]{:S(2)}) copy-start(bf16[8,1,128]{2,0,1:T(8,128)(2,1)} %param.20) | copy-start | bytes 6148
  2.5 4.4 %copy-start.2 = (bf16[8,1,1024,128]{3,2,1,0:T(8,128)(2,1)S(1)}, bf16[8,1,1024,128]{3,2,1,0:T(8,128)(2,1)}, u32[]{:S(2)}) copy-start(bf16[8,1,1024,128]{3,2,1,0:T(8,128)(2,1)} %param.18) | copy-start | bytes 6291460
  9.9 12.0 %copy-start.6 = (s32[256,8]{0,1:T(8,128)S(1)}, s32[256,8]{0,1:T(8,128)}, u32[]{:S(2)}) copy-start(s32[256,8]{0,1:T(8,128)} %param.27) | copy-start | bytes 24580
  9.9 12.3 %copy-start.5 = (bf16[256,128]{1,0:T(8,128)(2,1)S(1)}, bf16[256,128]{1,0:T(8,128)(2,1)}, u32[]{:S(2)}) copy-start(bf16[256,128]{1,0:T(8,128)(2,1)} %param.25) | copy-start | bytes 196612
  9.9 65.1 %all-to-all-start = ((bf16[128,1,8,2048]{3,2,1,0:T(8,128)(2,1)}), bf16[128,1,8,2048]{3,2,1,0:T(8,128)(2,1)}, u32[]{:S(2)}, u32[]{:S(2)}) async-start(bf16[128,1,8,2048]{3,2,1,0:T(8,128)(2,1)} %stack.3), calls=%async_computation | async-start | bytes 8388608 | tf_op jit(solution)/shard_map/all_to_all | solution.py:87
  123.1 2.2 copy-start.3
  196.7 5.5 %copy-start.4 = (f32[256,8]{0,1:T(8,128)S(1)}, f32[256,8]{0,1:T(8,128)}, u32[]{:S(2)}) copy-start(f32[256,8]{0,1:T(8,128)} %param.28) | copy-start | bytes 24580
  198.7 18.6 %all-to-all-start.3 = ((bf16[4,2,65536]{2,1,0:T(2,128)(2,1)}), bf16[4,2,65536]{2,1,0:T(2,128)(2,1)S(1)}, u32[]{:S(2)}, u32[]{:S(2)}) async-start(bf16[4,2,65536]{2,1,0:T(2,128)(2,1)} %reshape.303), calls=%async_computation.3 | async-start | bytes 2097152 | tf_op jit(solution)/shard_map/all_to_all | solution.py:126
  221.5 8.3 %copy-start.1 = (bf16[8192,128]{1,0:T(8,128)(2,1)S(1)}, bf16[8192,128]{1,0:T(8,128)(2,1)}, u32[]{:S(2)}) copy-start(bf16[8192,128]{1,0:T(8,128)(2,1)} %param.24) | copy-start | bytes 6291460
